TPU v7x, 32 devices: a whole 2x2x4 slice. The times are simulated.
32 devices in a mesh: dp: 16 (over z, x, core), tensor: 2 (over y).
Axes of the slice: x: 2, y: 2, z: 4, core: 2. Of those that a mesh axis runs over, the one named last changes fastest.
Arguments:
- context: bfloat16 [6144, 8192], P('dp', 'tensor'), may hold values from -6 to 6
- output_weight: bfloat16 [8192, 8192], P('tensor', 'dp'), may hold values from -0.0625 to 0.0625
- adapter_down_weight: bfloat16 [8192, 16], P('tensor'), may hold values from -0.0625 to 0.0625
- adapter_up_weight: bfloat16 [16, 8192], replicated, may hold values from -0.29882812 to 0.29882812
- residual: bfloat16 [6144, 8192], P('dp', 'tensor'), may hold values from -60 to 60
- frozen_residual_delta: bfloat16 [6144, 8192], P('dp', 'tensor'), may hold values from -6 to 6
- harmful_count: int32 [16], replicated, may hold values from 48 to 192
- retain_count: int32 [16], replicated, may hold values from 48 to 192
Outputs:
- adapted: bfloat16 [6144, 8192], P('dp', 'tensor')
- grad_a: float32 [8192, 16], P('tensor')
- grad_b: float32 [16, 8192], replicated
All inputs are finite; a program needn't handle non-finite values.
Results may differ from a plain program's by a relative error of at most 0.005.
Values may be sent and summed in bfloat16 or wider, within the bound.
No kernel may reach another device: no remote copies, remote signals or barrier semaphores. Data moves between devices by JAX's collectives and lax.ppermute only.
A program may use at most 192 MiB of HBM per device.

v0:
```python
import jax
import jax.numpy as jnp
from jax import lax
from jax.sharding import PartitionSpec as P

ADAPTER_SCALE = 2.0
NORM_EPS = 1e-06
REROUTE_WEIGHT = 65536.0
RETAIN_WEIGHT = 1024.0


def row_gradient(
    hidden_states,
    target,
    sq_state,
    sq_target,
    cross_term,
    gap_sq,
    harmful,
    retained,
    harm_total,
    keep_total,
):
    norm_h = jnp.sqrt(sq_state + NORM_EPS)
    norm_g = jnp.sqrt(sq_target + NORM_EPS)
    cosine = cross_term / (norm_h * norm_g)
    distance = jnp.sqrt(gap_sq + NORM_EPS)
    weight_harm = REROUTE_WEIGHT / harm_total * harmful
    weight_keep = RETAIN_WEIGHT / keep_total * retained
    first = (weight_harm / (norm_h * norm_g))[:, None] * target
    second = (weight_harm * cosine / (norm_h * norm_h))[:, None] * hidden_states
    third = (weight_keep / distance)[:, None] * (hidden_states - target)
    return first - second + third


def token_masks(positions, harm_here, keep_here):
    harmful = (positions < harm_here).astype(jnp.float32)
    retained = ((positions >= harm_here) & (positions < harm_here + keep_here)).astype(jnp.float32)
    return (harmful, retained)


def head_terms(context, output_weight):
    return jnp.dot(
        context,
        lax.all_gather(output_weight, "dp", axis=1, tiled=True),
        preferred_element_type=jnp.float32,
    )


def local(
    context,
    output_weight,
    adapter_down_weight,
    adapter_up_weight,
    residual,
    frozen_residual_delta,
    harmful_count,
    retain_count,
):
    seq_len = context.shape[0]
    tensor_rank = lax.axis_index("tensor")
    data_rank = lax.axis_index("dp")
    harm_total = jnp.sum(harmful_count).astype(jnp.float32)
    keep_total = jnp.sum(retain_count).astype(jnp.float32)
    harm_here = harmful_count[data_rank]
    keep_here = retain_count[data_rank]
    up_weight_single = adapter_up_weight.astype(jnp.float32)
    reduced_state = lax.psum(
        jnp.dot(context, adapter_down_weight, preferred_element_type=jnp.float32), "tensor"
    )
    attn_cols = lax.psum_scatter(
        head_terms(context, output_weight).astype(jnp.bfloat16),
        "tensor",
        scatter_dimension=1,
        tiled=True,
    ).astype(jnp.float32)
    col_count = attn_cols.shape[1]
    up_weight_columns = lax.dynamic_slice_in_dim(
        up_weight_single, tensor_rank * col_count, col_count, 1
    )
    hidden_states = (
        residual.astype(jnp.float32)
        + attn_cols
        + ADAPTER_SCALE * jnp.dot(reduced_state, up_weight_columns, precision=lax.Precision.HIGHEST)
    )
    target = residual.astype(jnp.float32) + frozen_residual_delta.astype(jnp.float32)
    gap = hidden_states - target
    sq_state, sq_target, cross_term, gap_sq = lax.psum(
        (
            jnp.sum(hidden_states * hidden_states, axis=1),
            jnp.sum(target * target, axis=1),
            jnp.sum(hidden_states * target, axis=1),
            jnp.sum(gap * gap, axis=1),
        ),
        "tensor",
    )
    positions = jnp.arange(seq_len, dtype=jnp.int32)
    harmful, retained = token_masks(positions, harm_here, keep_here)
    output_gradient = row_gradient(
        hidden_states,
        target,
        sq_state,
        sq_target,
        cross_term,
        gap_sq,
        harmful,
        retained,
        harm_total,
        keep_total,
    )
    reduced_gradient = lax.psum(
        ADAPTER_SCALE
        * jnp.dot(output_gradient, up_weight_columns.T, precision=lax.Precision.HIGHEST),
        "tensor",
    )
    local_a = jnp.dot(
        context.T,
        reduced_gradient,
        precision=lax.Precision.HIGHEST,
        preferred_element_type=jnp.float32,
    )
    shard_up_weight = ADAPTER_SCALE * jnp.dot(
        reduced_state.T, output_gradient, precision=lax.Precision.HIGHEST
    )
    grad_a, grad_b_cols = lax.psum((local_a, shard_up_weight), "dp")
    grad_b = lax.all_gather(grad_b_cols, "tensor", axis=1, tiled=True)
    adapted = hidden_states.astype(jnp.bfloat16)
    return (adapted, grad_a, grad_b)


def solution(mesh):
    return jax.shard_map(
        local,
        mesh=mesh,
        in_specs=(
            P("dp", "tensor"),
            P("tensor", "dp"),
            P("tensor", None),
            P(),
            P("dp", "tensor"),
            P("dp", "tensor"),
            P(),
            P(),
        ),
        out_specs=(P("dp", "tensor"), P("tensor", None), P()),
        check_vma=False,
    )
```

profile of v0, /device:TPU:0, one launch (start us, length us, event | category | flops | bytes accessed | tf_op | source)
XLA Modules:
  0.0 603.7 jit_solution(7466354331917010897)
XLA Ops:
  7.2 0.0 copy-start
  7.2 0.0 all-gather.2.cloned.1.call-start
  7.2 0.7 all-gather.2.cloned.1.call-update
  7.9 0.0 reduce-scatter.2.cloned.1.call-start
  8.0 330.5 %all-gather.2.cloned.1.call-done = bf16[4096,8192]{1,0:T(8,128)(2,1)} async-done(((bf16[4096,512]{1,0:T(8,128)(2,1)}), bf16[4096,8192]{1,0:T(8,128)(2,1)}) %all-gather.2.cloned.1.call-update) | async-done | bytes 67108880 | tf_op jit(solution)/shard_map/all_gather | solution.py:45
  338.4 0.0 copy-done
  338.4 33.6 %convolution_convert_fusion = bf16[384,8192]{1,0:T(8,128)(2,1)} fusion(bf16[384,4096]{1,0:T(8,128)(2,1)S(1)} %copy-done, bf16[4096,8192]{1,0:T(8,128)(2,1)} %all-gather.2.cloned.1.call-done), kind=kOutput, calls=%fused_computation | convolution fusion | flops 25772949504 | bytes 76546048 | tf_op jit(solution)/shard_map/dot_general | solution.py:43
  372.0 0.0 copy-start.3
  372.0 0.0 copy-start.4
  372.0 0.0 copy-start.1
  372.0 0.0 reduce-scatter.2.cloned.1.call-update
  372.0 0.0 all-reduce.4.cloned.1.call-start
  372.1 0.6 copy-done.3
  372.6 0.6 reduce_sum.58
  373.3 0.7 dynamic_slice.11
  373.9 0.0 copy-done.4
  373.9 0.6 reduce_sum.54
  374.6 0.6 dynamic_slice.10
  377.9 0.0 copy-done.1
  377.9 0.9 fusion.8
  378.8 8.7 %psum.56 = f32[384,16]{0,1:T(8,128)S(1)} all-reduce(f32[384,16]{0,1:T(8,128)S(1)} %fusion.8), channel_id=1, replica_groups=mesh['dp'=16,'tensor'=2] {'tensor'}, use_global_device_ids=true, to_apply=%region_1.0 | all-reduce | flops 6144 | bytes 49152 | tf_op jit(solution)/shard_map/psum | solution.py:68
  387.5 62.2 %reduce-scatter.2.cloned.1.call-done = bf16[384,4096]{1,0:T(8,128)(2,1)} async-done(((bf16[384,8192]{1,0:T(8,128)(2,1)}), bf16[384,4096]{1,0:T(8,128)(2,1)}) %reduce-scatter.2.cloned.1.call-update) | async-done | bytes 3145744 | tf_op jit(solution)/shard_map/reduce_scatter | solution.py:71
  449.8 10.0 %multiply_reduce_fusion.1 = (f32[384]{0:T(512)S(1)}, f32[384]{0:T(512)S(1)}, f32[384]{0:T(512)S(1)}, f32[384]{0:T(512)S(1)}, f32[384,4096]{1,0:T(8,128)}) fusion(bf16[384,4096]{1,0:T(8,128)(2,1)} %param.13, bf16[384,4096]{1,0:T(8,128)(2,1)} %param.12, f32[384,16]{0,1:T(8,128)S(1)} %psum.56, bf16[16,8192]{1,0:T(8,128)(2,1)} %param.11, s32[]{:T(128)S(6)} %select_n.7, ...), kind=kOutput, calls=%fused_computation.6 | convolution fusion | flops 327154176 | bytes 15890436 | tf_op jit(solution)/shard_map/dot_general | solution.py:84
  459.7 5.2 all-reduce.1
  464.9 0.7 select_divide_fusion
  465.5 0.0 copy-start.2
  465.6 9.2 %multiply_add_fusion = (f32[384,4096]{1,0:T(8,128)S(1)}, bf16[384,4096]{1,0:T(8,128)(2,1)}) fusion(f32[384,4096]{1,0:T(8,128)} %get-tuple-element.17, bf16[384,4096]{1,0:T(8,128)(2,1)} %param.13, bf16[384,4096]{1,0:T(8,128)(2,1)} %param.12, f32[384]{0:T(512)S(1)} %get-tuple-element.18, f32[384]{0:T(512)S(1)} %get-tuple-element.16, f32[384]{0:T(512)S(1)} %get-tuple-element.15), kind=kLoop, calls=%fused_computation.4 | loop fusion | flops 15728640 | bytes 22024704 | tf_op jit(solution)/shard_map/add | solution.py:33
  474.7 0.0 copy-done.2
  474.8 2.9 convolution_multiply_fusion.1
  477.7 3.8 convolution_multiply_fusion
  481.4 9.5 %psum.61 = f32[384,16]{1,0:T(8,128)S(1)} all-reduce(f32[384,16]{1,0:T(8,128)S(1)} %convolution_multiply_fusion.1), channel_id=1, replica_groups=mesh['dp'=16,'tensor'=2] {'tensor'}, use_global_device_ids=true, to_apply=%region_12.0 | all-reduce | flops 6144 | bytes 49152 | tf_op jit(solution)/shard_map/psum | solution.py:111
  490.9 2.1 convolution_bitcast_fusion
  493.0 0.0 all-reduce.4.cloned.1.call-update
  493.0 92.1 %all-reduce.4.cloned.1.call-done = (f32[4096,16]{0,1:T(8,128)}, f32[16,4096]{1,0:T(8,128)}) async-done(((f32[4096,16]{0,1:T(8,128)}, f32[16,4096]{1,0:T(8,128)}), (f32[4096,16]{0,1:T(8,128)}, f32[16,4096]{1,0:T(8,128)})) %all-reduce.4.cloned.1.call-update) | async-done | bytes 524304 | tf_op jit(solution)/shard_map/psum | solution.py:125
  585.1 9.6 %all_gather.7 = f32[16,8192]{1,0:T(8,128)S(1)} all-gather(f32[16,4096]{1,0:T(8,128)} %get-tuple-element.8), channel_id=1, replica_groups=mesh['dp'=16,'tensor'=2] {'tensor'}, dimensions={1}, use_global_device_ids=true | all-gather | bytes 786432 | tf_op jit(solution)/shard_map/all_gather | solution.py:126
  594.7 1.7 copy.14
  596.4 0.8 copy.15
Async XLA Ops:
  7.2 331.2 %copy-start = (bf16[384,4096]{1,0:T(8,128)(2,1)S(1)}, bf16[384,4096]{1,0:T(8,128)(2,1)}, u32[]{:S(2)}) copy-start(bf16[384,4096]{1,0:T(8,128)(2,1)} %param.8) | copy-start | bytes 9437188
  7.2 331.2 %all-gather.2.cloned.1.call-start = ((), (), s32[]{:S(2)}) async-start(), calls=%async_computation.1 | async-start | bytes 71303168 | tf_op jit(solution)/shard_map/all_gather | solution.py:45
  7.9 441.8 %reduce-scatter.2.cloned.1.call-start = ((), (), s32[]{:S(2)}) async-start(), calls=%async_computation.2 | async-start | bytes 9437184 | tf_op jit(solution)/shard_map/reduce_scatter | solution.py:71
  372.0 0.7 copy-start.3
  372.0 1.9 copy-start.4
  372.0 5.9 copy-start.1
  372.0 213.1 %all-reduce.4.cloned.1.call-start = ((), (), s32[]{:S(2)}) async-start(), calls=%async_computation.3 | async-start | bytes 1048576 | tf_op jit(solution)/shard_map/psum | solution.py:125
  465.5 9.2 %copy-start.2 = (bf16[16,8192]{1,0:T(8,128)(2,1)S(1)}, bf16[16,8192]{1,0:T(8,128)(2,1)}, u32[]{:S(2)}) copy-start(bf16[16,8192]{1,0:T(8,128)(2,1)} %param.11) | copy-start | bytes 786436
Sparse Core Ops, SparseCore 0:
  9.6 328.7 all-gather.1
  372.1 77.5 reduce-scatter.1
  493.1 91.9 all-reduce.3
where the time goes:
time: 604 us
  waiting for transfers between devices  486 us (80%)
  matrix products  53.2 us (9%)
  blocking collectives  33 us (5%)
  between operations  16.5 us (3%)
  other arithmetic  11.1 us (2%)
    all_gather x1, waiting for transfers between devices, head_terms(): lax.all_gather(output_weight, 'dp', axis=1, tiled=True)  330 us
    psum x1, waiting for transfers between devices, local(): grad_a, grad_b_cols = lax.psum((local_a, shard_up_weight), 'dp')  92.1 us
    reduce_scatter x1, waiting for transfers between devices, local(): lax.psum_scatter(head_terms(context, output_weight).astype(jnp.bfloat16),...  62.2 us
    dot_general x1, matrix products, head_terms(): jnp.dot(context, lax.all_gather(output_weight, 'dp', axis=1, tiled=True),...  33.6 us
  transfers between devices with their start and end apart: 3, of which 3 were waited for; matrix products, arithmetic and copies ran while one was open for 1% of the time, Pallas kernels for 0%

commit v1 on v0

v1 whole, which is shorter than its diff:
```python
import jax
import jax.numpy as jnp
from jax import lax
from jax.sharding import PartitionSpec as P

ADAPTER_SCALE = 2.0
NORM_EPS = 1e-06
REROUTE_WEIGHT = 65536.0
RETAIN_WEIGHT = 1024.0
INNER = 4
LAYERS = 4
LATE_CUTS = (256, 128, 128)
HIGHEST = lax.Precision.HIGHEST


def after(value, *earlier):
    return lax.optimization_barrier((value,) + earlier)[0]


def routes(step):
    pairs = []
    for z in range(LAYERS):
        for q in range(INNER):
            for t in range(2):
                to = step(z, q, t)
                if to is not None:
                    pairs.append(((z * INNER + q) * 2 + t, (to[0] * INNER + to[1]) * 2 + to[2]))
    return pairs


def send(value, step):
    return lax.ppermute(value, ("dp", "tensor"), routes(step))


def keeps_early(z, t):
    return (t == 0) == (z < 2)


def inward(z, q, t):
    return {0: (1, q, t), 3: (2, q, t)}.get(z)


def outward(z, q, t):
    return {1: (0, q, t), 2: (3, q, t)}.get(z)


def mid_swap(z, q, t):
    return {1: (2, q, t), 2: (1, q, t)}.get(z)


def inner_swap(bits, layers=range(LAYERS)):
    return lambda z, q, t: (z, q ^ bits, t) if z in layers else None


def to_early(z, q, t):
    return None if keeps_early(z, t) else (z, q, 1 - t)


def to_late(z, q, t):
    return (z, q, 1 - t) if keeps_early(z, t) else None


def among(early, bits):
    return lambda z, q, t: (z, q ^ bits, t) if keeps_early(z, t) == early else None


def dot_bf16(a, b):
    return jnp.dot(a, b, preferred_element_type=jnp.float32).astype(jnp.bfloat16)


def gather_rows(rows, layers):
    core = send(rows, inner_swap(1, layers))
    across = send(rows, inner_swap(2, layers))
    diagonal = send(across, inner_swap(1, layers))
    return jnp.concatenate([rows, core, across, diagonal], axis=0)


def add_bf16(a, b):
    return (a.astype(jnp.float32) + b.astype(jnp.float32)).astype(jnp.bfloat16)


def to_owners(block, early, rows):
    pieces = [block[:rows]]
    for bits in range(1, INNER):
        pieces.append(send(block[bits * rows : (bits + 1) * rows], among(early, bits)))
    return pieces


def line_attention(context, output_weight):
    rows = context.shape[0]
    cols = output_weight.shape[1]
    data_rank = lax.axis_index("dp")
    tensor_rank = lax.axis_index("tensor")
    layer = data_rank // INNER
    place = data_rank % INNER
    low = layer < 2
    at_end = (layer == 0) | (layer == LAYERS - 1)
    early = (tensor_rank == 0) == low

    guest_rows = send(context, inward)
    middle = send(output_weight, mid_swap)
    outer_end = send(output_weight, outward)
    own_all = gather_rows(context, range(LAYERS))

    cuts, start = [], 0
    for width in LATE_CUTS:
        cuts.append((start * cols // 512, (start + width) * cols // 512))
        start += width
    outer_mid, previous = [], guest_rows
    for lo, hi in cuts:
        previous = send(after(output_weight[:, lo:hi], previous), inward)
        outer_mid.append(previous)
    far, previous = [], middle
    for chunk in outer_mid:
        previous = send(after(chunk, previous), mid_swap)
        far.append(previous)
    guest_all = gather_rows(guest_rows, (1, 2))

    part_own = dot_bf16(own_all, output_weight)
    sum_own = add_bf16(part_own, send(part_own, to_early))
    own_pieces = to_owners(sum_own, True, rows)

    def late(chunk):
        back = send(dot_bf16(guest_all, chunk), outward)
        part = jnp.where(at_end, back, dot_bf16(own_all, chunk))
        total = add_bf16(part, send(part, to_late))
        return to_owners(total, False, rows)

    middle_pieces = late(middle)

    outer = jnp.where(at_end, outer_end, jnp.concatenate(outer_mid, axis=1))
    part_outer = dot_bf16(own_all, outer)
    sum_outer = add_bf16(part_outer, send(part_outer, to_early))
    outer_pieces = to_owners(sum_outer, True, rows)

    far_parts = [late(chunk) for chunk in far]
    far_pieces = [jnp.concatenate(group, axis=1) for group in zip(*far_parts)]

    first = [jnp.where(early, a, b) for a, b in zip(own_pieces, middle_pieces)]
    second = [jnp.where(early, a, b) for a, b in zip(outer_pieces, far_pieces)]
    stacked = jnp.stack(first + second)
    first_half = jnp.where(early, layer % 2, jnp.where(low, 0, 1))
    ordered = []
    for half in range(2):
        group = jnp.where(first_half == half, 0, INNER)
        for q in range(INNER):
            ordered.append(
                lax.dynamic_index_in_dim(stacked, group + (place ^ q), 0, keepdims=False)
            )
    return jnp.concatenate(ordered, axis=1)


def general_attention(context, output_weight):
    partial = dot_bf16(context, lax.all_gather(output_weight, "dp", axis=1, tiled=True))
    return lax.psum_scatter(partial, "tensor", scatter_dimension=1, tiled=True)


def line_swap(value, step):
    return send(value, step)


def line_sum_grads(grad_a_t, grad_b):
    data_rank = lax.axis_index("dp")
    tensor_rank = lax.axis_index("tensor")
    place = data_rank % INNER
    rank = grad_a_t.shape[0]
    both = jnp.concatenate([grad_a_t, grad_b], axis=0)
    for bits in (1, 2):
        half = both.shape[1] // 2
        upper = (place & bits) != 0
        low_part, high_part = both[:, :half], both[:, half:]
        keep = jnp.where(upper, high_part, low_part)
        give = jnp.where(upper, low_part, high_part)
        both = keep + send(give, inner_swap(bits))
    for bits in (1, 2):
        both = both + send(both, lambda z, q, t: (z ^ bits, q, t))
    other_b = send(both[rank:], lambda z, q, t: (z, q, 1 - t))
    both = jnp.concatenate([both, other_b], axis=0)
    for bits in (2, 1):
        upper = (place & bits) != 0
        got = send(both, inner_swap(bits))
        both = jnp.concatenate(
            [jnp.where(upper, got, both), jnp.where(upper, both, got)], axis=1
        )
    grad_a = both[:rank].T
    mine, other = both[rank : 2 * rank], both[2 * rank :]
    first = tensor_rank == 0
    grad_b = jnp.concatenate(
        [jnp.where(first, mine, other), jnp.where(first, other, mine)], axis=1
    )
    return grad_a, grad_b


def general_sum_grads(grad_a_t, grad_b):
    grad_a_t, grad_b = lax.psum((grad_a_t, grad_b), "dp")
    return grad_a_t.T, lax.all_gather(grad_b, "tensor", axis=1, tiled=True)


def solution(mesh):
    line = mesh.shape["dp"] == LAYERS * INNER and mesh.shape["tensor"] == 2

    def sum_tensor(value):
        if line:
            return value + send(value, lambda z, q, t: (z, q, 1 - t))
        return lax.psum(value, "tensor")

    def local(
        context,
        output_weight,
        adapter_down_weight,
        adapter_up_weight,
        residual,
        frozen_residual_delta,
        harmful_count,
        retain_count,
    ):
        seq_len = context.shape[0]
        tensor_rank = lax.axis_index("tensor")
        data_rank = lax.axis_index("dp")
        harm_total = jnp.sum(harmful_count).astype(jnp.float32)
        keep_total = jnp.sum(retain_count).astype(jnp.float32)
        harm_here = harmful_count[data_rank]
        keep_here = retain_count[data_rank]
        col_count = residual.shape[1]

        low_rank_t = sum_tensor(
            lax.dot_general(
                adapter_down_weight,
                context,
                (((0,), (1,)), ((), ())),
                preferred_element_type=jnp.float32,
            )
        )
        up_columns = lax.dynamic_slice_in_dim(
            adapter_up_weight, tensor_rank * col_count, col_count, 1
        ).astype(jnp.float32)
        low_up = ADAPTER_SCALE * lax.dot_general(
            low_rank_t, up_columns, (((0,), (0,)), ((), ())), precision=HIGHEST
        )
        target = residual.astype(jnp.float32) + frozen_residual_delta.astype(jnp.float32)

        attn = (line_attention if line else general_attention)(context, output_weight)
        states = residual.astype(jnp.float32) + attn.astype(jnp.float32) + low_up
        gap = states - target

        def on_up(values):
            return lax.dot_general(
                up_columns, values, (((1,), (1,)), ((), ())), precision=HIGHEST
            )

        sums = jnp.stack(
            [
                jnp.sum(states * states, axis=1),
                jnp.sum(target * target, axis=1),
                jnp.sum(states * target, axis=1),
                jnp.sum(gap * gap, axis=1),
            ]
        )
        rank = up_columns.shape[0]
        shared = sum_tensor(jnp.concatenate([on_up(states), on_up(target), sums], axis=0))
        states_up, target_up = shared[:rank], shared[rank : 2 * rank]
        sq_state, sq_target, cross_term, gap_sq = (shared[2 * rank + i] for i in range(4))

        positions = jnp.arange(seq_len, dtype=jnp.int32)
        harmful = (positions < harm_here).astype(jnp.float32)
        retained = (
            (positions >= harm_here) & (positions < harm_here + keep_here)
        ).astype(jnp.float32)
        norm_h = jnp.sqrt(sq_state + NORM_EPS)
        norm_g = jnp.sqrt(sq_target + NORM_EPS)
        cosine = cross_term / (norm_h * norm_g)
        distance = jnp.sqrt(gap_sq + NORM_EPS)
        weight_harm = REROUTE_WEIGHT / harm_total * harmful
        weight_keep = RETAIN_WEIGHT / keep_total * retained / distance
        on_target = weight_harm / (norm_h * norm_g) - weight_keep
        on_states = weight_keep - weight_harm * cosine / (norm_h * norm_h)

        cotangent = on_target[:, None] * target + on_states[:, None] * states
        low_cot_t = ADAPTER_SCALE * (on_target * target_up + on_states * states_up)
        grad_a_t = jnp.dot(low_cot_t, context.astype(jnp.float32), precision=HIGHEST)
        grad_b = ADAPTER_SCALE * jnp.dot(low_rank_t, cotangent, precision=HIGHEST)
        grad_a, grad_b = (line_sum_grads if line else general_sum_grads)(grad_a_t, grad_b)
        return states.astype(jnp.bfloat16), grad_a, grad_b

    return jax.shard_map(
        local,
        mesh=mesh,
        in_specs=(
            P("dp", "tensor"),
            P("tensor", "dp"),
            P("tensor", None),
            P(),
            P("dp", "tensor"),
            P("dp", "tensor"),
            P(),
            P(),
        ),
        out_specs=(P("dp", "tensor"), P("tensor", None), P()),
        check_vma=False,
    )
```

time: 604 us -> 583 us (0.965); the launches traced: 604 us -> 574 us
  waiting for transfers between devices: 486 us -> 258 us
  starting transfers between devices: 0.12 us -> 109 us
  matrix products: 53.2 us -> 122 us
  local copies, waits for them, and re-layouts: 4.3 us -> 61.4 us
  blocking collectives: 33 us -> 0 us
  between operations: 16.5 us -> 4.59 us
  other arithmetic: 11.1 us -> 19.2 us
    all_gather x1 -> x0, waiting for transfers between devices: 330 us -> none  [head_terms(): lax.all_gather(output_weight, 'dp', axis=1, tiled=True)]
    ppermute x0 -> x52, waiting for transfers between devices: none -> 258 us  [send(): return lax.ppermute(value, ('dp', 'tensor'), routes(step))]
    ppermute x0 -> x52, starting transfers between devices: none -> 109 us  [send(): return lax.ppermute(value, ('dp', 'tensor'), routes(step))]
    psum x1 -> x0, waiting for transfers between devices: 92.1 us -> none  [local(): grad_a, grad_b_cols = lax.psum((local_a, shard_up_weight), 'dp')]
    dot_general x6 -> x16, matrix products: 53.2 us -> 122 us  [the longest x10 93.7 us: dot_bf16(): jnp.dot(a, b, preferred_element_type=jnp.float32).astype(jnp.bfloat16)]
    reduce_scatter x1 -> x0, waiting for transfers between devices: 62.2 us -> none  [local(): lax.psum_scatter(head_terms(context, output_weight).astype(jnp.bfloat16),...]
    unnamed x12 -> x63, local copies, waits for them, and re-layouts: 3.06 us -> 31.4 us
    psum x3 -> x0, blocking collectives: 23.4 us -> none  [the longest x1 9.47 us: local(): lax.psum(ADAPTER_SCALE * jnp.dot(output_gradient, up_weight_columns.T, pr...]
  transfers between devices with their start and end apart: 3 -> 52, of which waited for: 3 -> 20; matrix products, arithmetic and copies ran while one was open for 1% -> 27% of each run, Pallas kernels for 0% -> 0%
where the time goes in v1:
time: 583 us; the launch traced here: 574 us
  waiting for transfers between devices  258 us (44%)
  matrix products  122 us (21%)
  starting transfers between devices  109 us (19%)
  local copies, waits for them, and re-layouts  61.4 us (11%)
  other arithmetic  19.2 us (3%)
    ppermute x52, waiting for transfers between devices, send(): return lax.ppermute(value, ('dp', 'tensor'), routes(step))  258 us
    ppermute x52, starting transfers between devices, send(): return lax.ppermute(value, ('dp', 'tensor'), routes(step))  109 us
    dot_general x10, matrix products, dot_bf16(): jnp.dot(a, b, preferred_element_type=jnp.float32).astype(jnp.bfloat16)  93.7 us
    unnamed x63, local copies, waits for them, and re-layouts  31.4 us
  transfers between devices with their start and end apart: 52, of which 20 were waited for; matrix products, arithmetic and copies ran while one was open for 27% of the time, Pallas kernels for 0%

profile of v1, /device:TPU:0, one launch (start us, length us, event | category | flops | bytes accessed | tf_op | source)
XLA Modules:
  0.0 573.7 jit_solution(10333493298070109793)
XLA Ops:
  0.6 3.0 collective-permute-start.1
  3.6 5.1 collective-permute-start.4
  11.5 2.9 fusion.65
  15.9 3.0 slice.131
  19.0 53.1 %collective-permute-done.1 = bf16[384,4096]{1,0:T(8,128)(2,1)} collective-permute-done((bf16[384,4096]{1,0:T(8,128)(2,1)}, bf16[384,4096]{1,0:T(8,128)(2,1)}, u32[]{:S(2)}, u32[]{:S(2)}) %collective-permute-start.1) | collective-permute-done | bytes 3145760 | tf_op jit(solution)/shard_map/ppermute | solution.py:32
  72.1 3.0 fusion.58
  75.1 5.4 collective-permute-start.18
  82.5 5.3 fusion.5
  91.2 3.9 constant_dynamic-update-slice_fusion.7
  95.1 3.9 constant_dynamic-update-slice_fusion.2
  99.0 3.9 constant_dynamic-update-slice_fusion.1
  102.9 22.1 %collective-permute-done.18 = bf16[4096,256]{1,0:T(8,128)(2,1)} collective-permute-done((bf16[4096,256]{1,0:T(8,128)(2,1)}, bf16[4096,256]{1,0:T(8,128)(2,1)}, u32[]{:S(2)}, u32[]{:S(2)}) %collective-permute-start.18) | collective-permute-done | bytes 2097184 | tf_op jit(solution)/shard_map/ppermute | solution.py:32
  126.3 7.5 %collective-permute-start.19 = (bf16[4096,128]{1,0:T(8,128)(2,1)}, bf16[4096,128]{1,0:T(8,128)(2,1)}, u32[]{:S(2)}, u32[]{:S(2)}) collective-permute-start(bf16[4096,128]{1,0:T(8,128)(2,1)} %get-tuple-element.10), channel_id=1, source_target_pairs={{0,8},{1,9},{2,10},{3,11},{4,12},{5,13},{6,14},{7,15},{24,16},{25,... | collective-permute-start | bytes 3145736 | tf_op jit(solution)/shard_map/ppermute | solution.py:32
  135.8 3.9 constant_dynamic-update-slice_fusion
  139.7 12.0 %convolution_convert_fusion.2 = bf16[1536,512]{0,1:T(8,128)(2,1)} fusion(bf16[1536,4096]{1,0:T(8,128)(2,1)} %constant_dynamic-update-slice_fusion, bf16[4096,512]{1,0:T(8,128)(2,1)} %param.9), kind=kOutput, calls=%fused_computation.28 | convolution fusion | flops 6443237376 | bytes 18350080 | tf_op jit(solution)/shard_map/dot_general | solution.py:68
  151.7 3.5 collective-permute-done.19
  156.4 5.4 collective-permute-start.20
  166.3 3.9 constant_dynamic-update-slice_fusion.5
  170.3 9.6 %convolution_convert_fusion = bf16[1536,512]{0,1:T(8,128)(2,1)} fusion(bf16[1536,4096]{1,0:T(8,128)(2,1)S(1)} %copy-done.1, bf16[4096,512]{1,0:T(8,128)(2,1)} %collective-permute-done.8), kind=kOutput, calls=%fused_computation.26 | convolution fusion | flops 6443237376 | bytes 18350080 | tf_op jit(solution)/shard_map/dot_general | solution.py:68
  179.9 39.6 %collective-permute-done.17 = bf16[4096,512]{1,0:T(8,128)(2,1)} collective-permute-done((bf16[4096,512]{1,0:T(8,128)(2,1)}, bf16[4096,512]{1,0:T(8,128)(2,1)}, u32[]{:S(2)}, u32[]{:S(2)}) %collective-permute-start.17) | collective-permute-done | bytes 4194336 | tf_op jit(solution)/shard_map/ppermute | solution.py:32
  219.4 13.4 %fusion.17 = bf16[1536,512]{0,1:T(8,128)(2,1)} fusion(bf16[1536,4096]{1,0:T(8,128)(2,1)} %constant_dynamic-update-slice_fusion, bf16[4096,512]{1,0:T(8,128)(2,1)} %collective-permute-done.17, bf16[4096,128]{1,0:T(8,128)(2,1)} %collective-permute-done.20, bf16[4096,128]{1,0:T(8,128)(2,1)} %collective-permute-done.19, ...), kind=kOutput, calls=%fused_computation.25 | convolution fusion | flops 6457917440 | bytes 22544384 | tf_op jit(solution)/shard_map/dot_general | solution.py:68
  235.0 9.5 %convolution_convert_fusion.3 = bf16[1536,256]{0,1:T(8,128)(2,1)} fusion(bf16[1536,4096]{1,0:T(8,128)(2,1)} %constant_dynamic-update-slice_fusion, bf16[4096,256]{1,0:T(8,128)(2,1)} %collective-permute-done.22), kind=kOutput, calls=%fused_computation.29 | convolution fusion | flops 3221618688 | bytes 15466496 | tf_op jit(solution)/shard_map/dot_general | solution.py:68
  250.6 3.7 collective-permute-start.13
  256.4 9.6 %convolution_convert_fusion.7 = bf16[1536,128]{0,1:T(8,128)(2,1)} fusion(bf16[1536,4096]{1,0:T(8,128)(2,1)} %constant_dynamic-update-slice_fusion, bf16[4096,128]{1,0:T(8,128)(2,1)S(1)} %collective-permute-done.25), kind=kOutput, calls=%fused_computation.33 | convolution fusion | flops 1610809344 | bytes 14024704 | tf_op jit(solution)/shard_map/dot_general | solution.py:68
  266.0 4.4 collective-permute-done.21
  273.8 6.3 %convolution_convert_fusion.5 = bf16[1536,128]{0,1:T(8,128)(2,1)} fusion(bf16[1536,4096]{1,0:T(8,128)(2,1)S(1)} %bitcast.72, bf16[4096,128]{1,0:T(8,128)(2,1)} %collective-permute-done.28), kind=kOutput, calls=%fused_computation.31 | convolution fusion | flops 1610809344 | bytes 14024704 | tf_op jit(solution)/shard_map/dot_general | solution.py:68
  280.1 4.0 constant_dynamic-update-slice_fusion.4
  284.0 12.1 %convolution_convert_fusion.1 = bf16[1536,512]{0,1:T(8,128)(2,1)} fusion(bf16[1536,4096]{1,0:T(8,128)(2,1)} %constant_dynamic-update-slice_fusion.4, bf16[4096,512]{1,0:T(8,128)(2,1)} %collective-permute-done.8), kind=kOutput, calls=%fused_computation.27 | convolution fusion | flops 6443237376 | bytes 18350080 | tf_op jit(solution)/shard_map/dot_general | solution.py:68
  297.6 6.3 %convolution_convert_fusion.6 = bf16[1536,128]{0,1:T(8,128)(2,1)} fusion(bf16[1536,4096]{1,0:T(8,128)(2,1)S(1)} %copy-done.2, bf16[4096,128]{1,0:T(8,128)(2,1)} %collective-permute-done.28), kind=kOutput, calls=%fused_computation.32 | convolution fusion | flops 1610809344 | bytes 14024704 | tf_op jit(solution)/shard_map/dot_general | solution.py:68
  305.2 6.3 %convolution_convert_fusion.8 = bf16[1536,128]{0,1:T(8,128)(2,1)} fusion(bf16[1536,4096]{1,0:T(8,128)(2,1)S(1)} %copy-done.2, bf16[4096,128]{1,0:T(8,128)(2,1)} %copy-done.9), kind=kOutput, calls=%fused_computation.34 | convolution fusion | flops 1610809344 | bytes 14024704 | tf_op jit(solution)/shard_map/dot_general | solution.py:68
  312.9 8.6 %convolution_convert_fusion.4 = bf16[1536,256]{0,1:T(8,128)(2,1)S(1)} fusion(bf16[1536,4096]{1,0:T(8,128)(2,1)} %constant_dynamic-update-slice_fusion.4, bf16[4096,256]{1,0:T(8,128)(2,1)} %collective-permute-done.22), kind=kOutput, calls=%fused_computation.30 | convolution fusion | flops 3221618688 | bytes 15466496 | tf_op jit(solution)/shard_map/dot_general | solution.py:68
  321.5 32.9 %collective-permute-done.29 = bf16[1536,128]{0,1:T(8,128)(2,1)} collective-permute-done((bf16[1536,128]{0,1:T(8,128)(2,1)}, bf16[1536,128]{0,1:T(8,128)(2,1)}, u32[]{:S(2)}, u32[]{:S(2)}) %collective-permute-start.29) | collective-permute-done | bytes 393248 | tf_op jit(solution)/shard_map/ppermute | solution.py:32
  356.8 6.0 %collective-permute-done.26 = bf16[1536,128]{0,1:T(8,128)(2,1)S(1)} collective-permute-done((bf16[1536,128]{0,1:T(8,128)(2,1)}, bf16[1536,128]{0,1:T(8,128)(2,1)S(1)}, u32[]{:S(2)}, u32[]{:S(2)}) %collective-permute-start.26) | collective-permute-done | bytes 393248 | tf_op jit(solution)/shard_map/ppermute | solution.py:32
  365.0 11.0 %collective-permute-done.23 = bf16[1536,256]{0,1:T(8,128)(2,1)S(1)} collective-permute-done((bf16[1536,256]{0,1:T(8,128)(2,1)S(1)}, bf16[1536,256]{0,1:T(8,128)(2,1)S(1)}, u32[]{:S(2)}, u32[]{:S(2)}) %collective-permute-start.23) | collective-permute-done | bytes 786464 | tf_op jit(solution)/shard_map/ppermute | solution.py:32
  382.6 4.8 collective-permute-done.27
  389.7 14.6 %collective-permute-done.24 = bf16[1536,256]{0,1:T(8,128)(2,1)S(1)} collective-permute-done((bf16[1536,256]{0,1:T(8,128)(2,1)S(1)}, bf16[1536,256]{0,1:T(8,128)(2,1)S(1)}, u32[]{:S(2)}, u32[]{:S(2)}) %collective-permute-start.24) | collective-permute-done | bytes 786464 | tf_op jit(solution)/shard_map/ppermute | solution.py:32
  404.4 28.8 %collective-permute-done.10 = bf16[1536,512]{0,1:T(8,128)(2,1)S(1)} collective-permute-done((bf16[1536,512]{0,1:T(8,128)(2,1)S(1)}, bf16[1536,512]{0,1:T(8,128)(2,1)S(1)}, u32[]{:S(2)}, u32[]{:S(2)}) %collective-permute-start.10) | collective-permute-done | bytes 1572896 | tf_op jit(solution)/shard_map/ppermute | solution.py:32
  440.4 3.7 collective-permute-start.35
  456.4 5.6 collective-permute-done.39
  482.4 9.2 %multiply_reduce_fusion = (f32[384]{0:T(512)S(1)}, f32[384]{0:T(512)S(1)}, f32[384]{0:T(512)S(1)}, f32[384]{0:T(512)S(1)}, bf16[384,4096]{1,0:T(8,128)(2,1)}, /*index=5*/f32[384,4096]{1,0:T(8,128)S(1)}) fusion(bf16[384,4096]{1,0:T(8,128)(2,1)S(1)} %copy-done.7, bf16[384,4096]{1,0:T(8,128)(2,1)} %param.12, f32[16,384]{1,0:T(8,128)S(1)} %add.183, ...), kind=kOutput, calls=%fused_computation.7 | convolution fusion | flops 328727040 | bytes 19036164 | tf_op jit(solution)/shard_map/dot_general | solution.py:237
  491.6 2.9 fusion.33
  495.8 25.2 %collective-permute-start.44 = (f32[36,384]{1,0:T(8,128)S(1)}, f32[36,384]{1,0:T(8,128)}, u32[]{:S(2)}, u32[]{:S(2)}) collective-permute-start(f32[36,384]{1,0:T(8,128)S(1)} %concatenate.50), channel_id=1, source_target_pairs={{0,1},{1,0},{2,3},{3,2},{4,5},{5,4},{6,7},{7,6},{8,9},{9,8},{10,11... | collective-permute-start | bytes 165896 | tf_op jit(solution)/shard_map/ppermute | solution.py:32
  531.0 6.9 %fusion.6 = f32[16,4096]{1,0:T(8,128)S(1)} fusion(f32[16,384]{1,0:T(8,128)S(1)} %add.183, f32[384,4096]{1,0:T(8,128)} %copy-done.5, bf16[384,4096]{1,0:T(8,128)(2,1)S(1)} %copy-done.7, bf16[384,4096]{1,0:T(8,128)(2,1)} %param.12, f32[384]{0:T(512)S(1)} %get-tuple-element.65, f32[384]{0:T(512)S(1)} %get-tuple-element.64), kind=kOutput, calls=%fused_computation.12 | convolution fusion | flops 311492608 | bytes 12872704 | tf_op jit(solution)/shard_map/dot_general | solution.py:281
  542.4 5.1 collective-permute-done.46
  547.7 5.0 collective-permute-done.47
  553.1 6.6 %collective-permute-done.48 = f32[32,1024]{1,0:T(8,128)S(1)} collective-permute-done((f32[32,1024]{1,0:T(8,128)S(1)}, f32[32,1024]{1,0:T(8,128)S(1)}, u32[]{:S(2)}, u32[]{:S(2)}) %collective-permute-start.48) | collective-permute-done | bytes 131104 | tf_op jit(solution)/shard_map/ppermute | solution.py:32
  560.1 4.0 collective-permute-done.49
  564.6 5.2 collective-permute-done.50
  (200 shorter events, 107.5 us)
Async XLA Ops:
  0.6 71.4 %collective-permute-start.1 = (bf16[384,4096]{1,0:T(8,128)(2,1)}, bf16[384,4096]{1,0:T(8,128)(2,1)}, u32[]{:S(2)}, u32[]{:S(2)}) collective-permute-start(bf16[384,4096]{1,0:T(8,128)(2,1)} %param.8), channel_id=1, source_target_pairs={{0,4},{1,5},{2,6},{3,7},{4,0},{5,1},{6,2},{7,3},{8,12},{9,13},{10,... | collective-permute-start | bytes 9437192 | tf_op jit(solution)/shard_map/ppermute | solution.py:32
  3.6 71.5 %collective-permute-start.4 = (bf16[384,4096]{1,0:T(8,128)(2,1)}, bf16[384,4096]{1,0:T(8,128)(2,1)}, u32[]{:S(2)}, u32[]{:S(2)}) collective-permute-start(bf16[384,4096]{1,0:T(8,128)(2,1)} %param.8), channel_id=1, source_target_pairs={{0,8},{1,9},{2,10},{3,11},{4,12},{5,13},{6,14},{7,15},{24,16},{25,... | collective-permute-start | bytes 9437192 | tf_op jit(solution)/shard_map/ppermute | solution.py:32
  8.8 80.0 %collective-permute-start = (bf16[384,4096]{1,0:T(8,128)(2,1)}, bf16[384,4096]{1,0:T(8,128)(2,1)}, u32[]{:S(2)}, u32[]{:S(2)}) collective-permute-start(bf16[384,4096]{1,0:T(8,128)(2,1)} %param.8), channel_id=1, source_target_pairs={{0,2},{1,3},{2,0},{3,1},{4,6},{5,7},{6,4},{7,5},{8,10},{9,11},{10,... | collective-permute-start | bytes 9437192 | tf_op jit(solution)/shard_map/ppermute | solution.py:32
  8.8 117.5 %collective-permute-start.8 = (bf16[4096,512]{1,0:T(8,128)(2,1)}, bf16[4096,512]{1,0:T(8,128)(2,1)}, u32[]{:S(2)}, u32[]{:S(2)}) collective-permute-start(bf16[4096,512]{1,0:T(8,128)(2,1)} %param.9), channel_id=1, source_target_pairs={{8,16},{9,17},{10,18},{11,19},{12,20},{13,21},{14,22},{15,23},{16,... | collective-permute-start | bytes 12582920 | tf_op jit(solution)/shard_map/ppermute | solution.py:32
  14.4 73.5 %collective-permute-start.43 = (f32[16,384]{1,0:T(8,128)S(1)}, f32[16,384]{1,0:T(8,128)S(1)}, u32[]{:S(2)}, u32[]{:S(2)}) collective-permute-start(f32[16,384]{1,0:T(8,128)S(1)} %fusion.65), channel_id=1, source_target_pairs={{0,1},{1,0},{2,3},{3,2},{4,5},{5,4},{6,7},{7,6},{8,9},{9,8},{10,11... | collective-permute-start | bytes 73736 | tf_op jit(solution)/shard_map/ppermute | solution.py:32
  72.1 61.7 %collective-permute-start.2 = (bf16[384,4096]{1,0:T(8,128)(2,1)}, bf16[384,4096]{1,0:T(8,128)(2,1)}, u32[]{:S(2)}, u32[]{:S(2)}) collective-permute-start(bf16[384,4096]{1,0:T(8,128)(2,1)} %collective-permute-done.1), channel_id=1, source_target_pairs={{0,2},{1,3},{2,0},{3,1},{4,6},{5,7},{6,4},{7,5},{8,10},{9,11},{10,... | collective-permute-start | bytes 9437192 | tf_op jit(solution)/shard_map/ppermute | solution.py:32
  75.1 49.8 %collective-permute-start.18 = (bf16[4096,256]{1,0:T(8,128)(2,1)}, bf16[4096,256]{1,0:T(8,128)(2,1)}, u32[]{:S(2)}, u32[]{:S(2)}) collective-permute-start(bf16[4096,256]{1,0:T(8,128)(2,1)} %slice.131), channel_id=1, source_target_pairs={{0,8},{1,9},{2,10},{3,11},{4,12},{5,13},{6,14},{7,15},{24,16},{25,... | collective-permute-start | bytes 6291464 | tf_op jit(solution)/shard_map/ppermute | solution.py:32
  87.9 68.5 %collective-permute-start.5 = (bf16[384,4096]{1,0:T(8,128)(2,1)}, bf16[384,4096]{1,0:T(8,128)(2,1)S(1)}, u32[]{:S(2)}, u32[]{:S(2)}) collective-permute-start(bf16[384,4096]{1,0:T(8,128)(2,1)} %collective-permute-done.4), channel_id=1, source_target_pairs={{8,10},{9,11},{10,8},{11,9},{12,14},{13,15},{14,12},{15,13},{16,18... | collective-permute-start | bytes 9437192 | tf_op jit(solution)/shard_map/ppermute | solution.py:32
  88.8 73.1 %collective-permute-start.6 = (bf16[384,4096]{1,0:T(8,128)(2,1)}, bf16[384,4096]{1,0:T(8,128)(2,1)}, u32[]{:S(2)}, u32[]{:S(2)}) collective-permute-start(bf16[384,4096]{1,0:T(8,128)(2,1)} %collective-permute-done.4), channel_id=1, source_target_pairs={{8,12},{9,13},{10,14},{11,15},{12,8},{13,9},{14,10},{15,11},{16,20... | collective-permute-start | bytes 9437192 | tf_op jit(solution)/shard_map/ppermute | solution.py:32
  125.0 94.5 %collective-permute-start.17 = (bf16[4096,512]{1,0:T(8,128)(2,1)}, bf16[4096,512]{1,0:T(8,128)(2,1)}, u32[]{:S(2)}, u32[]{:S(2)}) collective-permute-start(bf16[4096,512]{1,0:T(8,128)(2,1)} %param.9), channel_id=1, source_target_pairs={{8,0},{9,1},{10,2},{11,3},{12,4},{13,5},{14,6},{15,7},{16,24},{17,... | collective-permute-start | bytes 12582920 | tf_op jit(solution)/shard_map/ppermute | solution.py:32
  126.3 28.9 %collective-permute-start.19 = (bf16[4096,128]{1,0:T(8,128)(2,1)}, bf16[4096,128]{1,0:T(8,128)(2,1)}, u32[]{:S(2)}, u32[]{:S(2)}) collective-permute-start(bf16[4096,128]{1,0:T(8,128)(2,1)} %get-tuple-element.10), channel_id=1, source_target_pairs={{0,8},{1,9},{2,10},{3,11},{4,12},{5,13},{6,14},{7,15},{24,16},{25,... | collective-permute-start | bytes 3145736 | tf_op jit(solution)/shard_map/ppermute | solution.py:32
  133.7 100.5 %collective-permute-start.22 = (bf16[4096,256]{1,0:T(8,128)(2,1)}, bf16[4096,256]{1,0:T(8,128)(2,1)}, u32[]{:S(2)}, u32[]{:S(2)}) collective-permute-start(bf16[4096,256]{1,0:T(8,128)(2,1)} %collective-permute-done.18), channel_id=1, source_target_pairs={{8,16},{9,17},{10,18},{11,19},{12,20},{13,21},{14,22},{15,23},{16,... | collective-permute-start | bytes 6291464 | tf_op jit(solution)/shard_map/ppermute | solution.py:32
  155.1 89.4 %collective-permute-start.3 = (bf16[1536,512]{0,1:T(8,128)(2,1)}, bf16[1536,512]{0,1:T(8,128)(2,1)}, u32[]{:S(2)}, u32[]{:S(2)}) collective-permute-start(bf16[1536,512]{0,1:T(8,128)(2,1)} %convolution_convert_fusion.2), channel_id=1, source_target_pairs={{1,0},{3,2},{5,4},{7,6},{9,8},{11,10},{13,12},{15,14},{16,17},{18,... | collective-permute-start | bytes 4718600 | tf_op jit(solution)/shard_map/ppermute | solution.py:32
  156.4 63.0 %collective-permute-start.20 = (bf16[4096,128]{1,0:T(8,128)(2,1)}, bf16[4096,128]{1,0:T(8,128)(2,1)}, u32[]{:S(2)}, u32[]{:S(2)}) collective-permute-start(bf16[4096,128]{1,0:T(8,128)(2,1)} %get-tuple-element.11), channel_id=1, source_target_pairs={{0,8},{1,9},{2,10},{3,11},{4,12},{5,13},{6,14},{7,15},{24,16},{25,... | collective-permute-start | bytes 3145736 | tf_op jit(solution)/shard_map/ppermute | solution.py:32
  161.8 118.2 %collective-permute-start.7 = (bf16[384,4096]{1,0:T(8,128)(2,1)}, bf16[384,4096]{1,0:T(8,128)(2,1)}, u32[]{:S(2)}, u32[]{:S(2)}) collective-permute-start(bf16[384,4096]{1,0:T(8,128)(2,1)} %collective-permute-done.6), channel_id=1, source_target_pairs={{8,10},{9,11},{10,8},{11,9},{12,14},{13,15},{14,12},{15,13},{16,18... | collective-permute-start | bytes 9437192 | tf_op jit(solution)/shard_map/ppermute | solution.py:32
  232.8 37.5 %collective-permute-start.21 = (bf16[1536,512]{0,1:T(8,128)(2,1)}, bf16[1536,512]{0,1:T(8,128)(2,1)}, u32[]{:S(2)}, u32[]{:S(2)}) collective-permute-start(bf16[1536,512]{0,1:T(8,128)(2,1)} %fusion.17), channel_id=1, source_target_pairs={{1,0},{3,2},{5,4},{7,6},{9,8},{11,10},{13,12},{15,14},{16,17},{18,... | collective-permute-start | bytes 4718600 | tf_op jit(solution)/shard_map/ppermute | solution.py:32
  234.3 20.1 %collective-permute-start.25 = (bf16[4096,128]{1,0:T(8,128)(2,1)}, bf16[4096,128]{1,0:T(8,128)(2,1)S(1)}, u32[]{:S(2)}, u32[]{:S(2)}) collective-permute-start(bf16[4096,128]{1,0:T(8,128)(2,1)} %collective-permute-done.19), channel_id=1, source_target_pairs={{8,16},{9,17},{10,18},{11,19},{12,20},{13,21},{14,22},{15,23},{16,... | collective-permute-start | bytes 3145736 | tf_op jit(solution)/shard_map/ppermute | solution.py:32
  248.6 188.0 %collective-permute-start.11 = (bf16[384,512]{0,1:T(8,128)(2,1)}, bf16[384,512]{0,1:T(8,128)(2,1)}, u32[]{:S(2)}, u32[]{:S(2)}) collective-permute-start(bf16[384,512]{0,1:T(8,128)(2,1)} %get-tuple-element.44), channel_id=1, source_target_pairs={{0,2},{2,0},{4,6},{6,4},{8,10},{10,8},{12,14},{14,12},{17,19},{19,... | collective-permute-start | bytes 1179656 | tf_op jit(solution)/shard_map/ppermute | solution.py:32
  250.6 189.8 %collective-permute-start.13 = (bf16[384,512]{0,1:T(8,128)(2,1)}, bf16[384,512]{0,1:T(8,128)(2,1)}, u32[]{:S(2)}, u32[]{:S(2)}) collective-permute-start(bf16[384,512]{0,1:T(8,128)(2,1)} %get-tuple-element.43), channel_id=1, source_target_pairs={{0,4},{2,6},{4,0},{6,2},{8,12},{10,14},{12,8},{14,10},{17,21},{19,... | collective-permute-start | bytes 1179656 | tf_op jit(solution)/shard_map/ppermute | solution.py:32
  254.4 19.4 %collective-permute-start.28 = (bf16[4096,128]{1,0:T(8,128)(2,1)}, bf16[4096,128]{1,0:T(8,128)(2,1)}, u32[]{:S(2)}, u32[]{:S(2)}) collective-permute-start(bf16[4096,128]{1,0:T(8,128)(2,1)} %collective-permute-done.20), channel_id=1, source_target_pairs={{8,16},{9,17},{10,18},{11,19},{12,20},{13,21},{14,22},{15,23},{16,... | collective-permute-start | bytes 3145736 | tf_op jit(solution)/shard_map/ppermute | solution.py:32
  296.1 81.8 %collective-permute-start.9 = (bf16[1536,512]{0,1:T(8,128)(2,1)}, bf16[1536,512]{0,1:T(8,128)(2,1)}, u32[]{:S(2)}, u32[]{:S(2)}) collective-permute-start(bf16[1536,512]{0,1:T(8,128)(2,1)} %convolution_convert_fusion.1), channel_id=1, source_target_pairs={{8,0},{9,1},{10,2},{11,3},{12,4},{13,5},{14,6},{15,7},{16,24},{17,... | collective-permute-start | bytes 4718600 | tf_op jit(solution)/shard_map/ppermute | solution.py:32
  303.9 50.6 %collective-permute-start.29 = (bf16[1536,128]{0,1:T(8,128)(2,1)}, bf16[1536,128]{0,1:T(8,128)(2,1)}, u32[]{:S(2)}, u32[]{:S(2)}) collective-permute-start(bf16[1536,128]{0,1:T(8,128)(2,1)} %convolution_convert_fusion.6), channel_id=1, source_target_pairs={{8,0},{9,1},{10,2},{11,3},{12,4},{13,5},{14,6},{15,7},{16,24},{17,... | collective-permute-start | bytes 1179656 | tf_op jit(solution)/shard_map/ppermute | solution.py:32
  311.5 51.3 %collective-permute-start.26 = (bf16[1536,128]{0,1:T(8,128)(2,1)}, bf16[1536,128]{0,1:T(8,128)(2,1)S(1)}, u32[]{:S(2)}, u32[]{:S(2)}) collective-permute-start(bf16[1536,128]{0,1:T(8,128)(2,1)} %convolution_convert_fusion.8), channel_id=1, source_target_pairs={{8,0},{9,1},{10,2},{11,3},{12,4},{13,5},{14,6},{15,7},{16,24},{17,... | collective-permute-start | bytes 1179656 | tf_op jit(solution)/shard_map/ppermute | solution.py:32
  354.4 21.6 %collective-permute-start.23 = (bf16[1536,256]{0,1:T(8,128)(2,1)S(1)}, bf16[1536,256]{0,1:T(8,128)(2,1)S(1)}, u32[]{:S(2)}, u32[]{:S(2)}) collective-permute-start(bf16[1536,256]{0,1:T(8,128)(2,1)S(1)} %convolution_convert_fusion.4), channel_id=1, source_target_pairs={{8,0},{9,1},{10,2},{11,3},{12,4},{13,5},{14,6},{15,7},{16,24},{17,... | collective-permute-start | bytes 2359304 | tf_op jit(solution)/shard_map/ppermute | solution.py:32
  362.8 18.3 %collective-permute-start.30 = (bf16[1536,128]{0,1:T(8,128)(2,1)S(1)}, bf16[1536,128]{0,1:T(8,128)(2,1)S(1)}, u32[]{:S(2)}, u32[]{:S(2)}) collective-permute-start(bf16[1536,128]{0,1:T(8,128)(2,1)S(1)} %broadcast_select_fusion.2), channel_id=1, source_target_pairs={{0,1},{2,3},{4,5},{6,7},{8,9},{10,11},{12,13},{14,15},{17,16},{19,... | collective-permute-start | bytes 1179656 | tf_op jit(solution)/shard_map/ppermute | solution.py:32
  376.0 11.3 %collective-permute-start.27 = (bf16[1536,128]{0,1:T(8,128)(2,1)S(1)}, bf16[1536,128]{0,1:T(8,128)(2,1)S(1)}, u32[]{:S(2)}, u32[]{:S(2)}) collective-permute-start(bf16[1536,128]{0,1:T(8,128)(2,1)S(1)} %broadcast_select_fusion.3), channel_id=1, source_target_pairs={{0,1},{2,3},{4,5},{6,7},{8,9},{10,11},{12,13},{14,15},{17,16},{19,... | collective-permute-start | bytes 1179656 | tf_op jit(solution)/shard_map/ppermute | solution.py:32
  378.0 26.3 %collective-permute-start.24 = (bf16[1536,256]{0,1:T(8,128)(2,1)S(1)}, bf16[1536,256]{0,1:T(8,128)(2,1)S(1)}, u32[]{:S(2)}, u32[]{:S(2)}) collective-permute-start(bf16[1536,256]{0,1:T(8,128)(2,1)S(1)} %broadcast_select_fusion.1), channel_id=1, source_target_pairs={{0,1},{2,3},{4,5},{6,7},{8,9},{10,11},{12,13},{14,15},{17,16},{19,... | collective-permute-start | bytes 2359304 | tf_op jit(solution)/shard_map/ppermute | solution.py:32
  381.1 52.2 %collective-permute-start.10 = (bf16[1536,512]{0,1:T(8,128)(2,1)S(1)}, bf16[1536,512]{0,1:T(8,128)(2,1)S(1)}, u32[]{:S(2)}, u32[]{:S(2)}) collective-permute-start(bf16[1536,512]{0,1:T(8,128)(2,1)S(1)} %broadcast_select_fusion), channel_id=1, source_target_pairs={{0,1},{2,3},{4,5},{6,7},{8,9},{10,11},{12,13},{14,15},{17,16},{19,... | collective-permute-start | bytes 4718600 | tf_op jit(solution)/shard_map/ppermute | solution.py:32
  387.4 58.5 %collective-permute-start.15 = (bf16[384,512]{0,1:T(8,128)(2,1)S(1)}, bf16[384,512]{0,1:T(8,128)(2,1)S(1)}, u32[]{:S(2)}, u32[]{:S(2)}) collective-permute-start(bf16[384,512]{0,1:T(8,128)(2,1)S(1)} %copy-done.21), channel_id=1, source_target_pairs={{0,6},{2,4},{4,2},{6,0},{8,14},{10,12},{12,10},{14,8},{17,23},{19,... | collective-permute-start | bytes 1179656 | tf_op jit(solution)/shard_map/ppermute | solution.py:32
  433.7 4.8 collective-permute-start.12
  434.7 9.4 %collective-permute-start.14 = (bf16[384,512]{0,1:T(8,128)(2,1)S(1)}, bf16[384,512]{0,1:T(8,128)(2,1)S(1)}, u32[]{:S(2)}, u32[]{:S(2)}) collective-permute-start(bf16[384,512]{0,1:T(8,128)(2,1)S(1)} %get-tuple-element.40), channel_id=1, source_target_pairs={{1,5},{3,7},{5,1},{7,3},{9,13},{11,15},{13,9},{15,11},{16,20},{18,... | collective-permute-start | bytes 1179656 | tf_op jit(solution)/shard_map/ppermute | solution.py:32
  436.6 11.0 %collective-permute-start.31 = (bf16[384,512]{0,1:T(8,128)(2,1)S(1)}, bf16[384,512]{0,1:T(8,128)(2,1)S(1)}, u32[]{:S(2)}, u32[]{:S(2)}) collective-permute-start(bf16[384,512]{0,1:T(8,128)(2,1)S(1)} %copy-done.20), channel_id=1, source_target_pairs={{0,2},{2,0},{4,6},{6,4},{8,10},{10,8},{12,14},{14,12},{17,19},{19,... | collective-permute-start | bytes 1179656 | tf_op jit(solution)/shard_map/ppermute | solution.py:32
  438.5 8.1 %collective-permute-start.16 = (bf16[384,512]{0,1:T(8,128)(2,1)S(1)}, bf16[384,512]{0,1:T(8,128)(2,1)S(1)}, u32[]{:S(2)}, u32[]{:S(2)}) collective-permute-start(bf16[384,512]{0,1:T(8,128)(2,1)S(1)} %get-tuple-element.39), channel_id=1, source_target_pairs={{1,7},{3,5},{5,3},{7,1},{9,15},{11,13},{13,11},{15,9},{16,22},{18,... | collective-permute-start | bytes 1179656 | tf_op jit(solution)/shard_map/ppermute | solution.py:32
  440.4 13.8 %collective-permute-start.35 = (bf16[384,512]{0,1:T(8,128)(2,1)S(1)}, bf16[384,512]{0,1:T(8,128)(2,1)S(1)}, u32[]{:S(2)}, u32[]{:S(2)}) collective-permute-start(bf16[384,512]{0,1:T(8,128)(2,1)S(1)} %copy-done.19), channel_id=1, source_target_pairs={{0,4},{2,6},{4,0},{6,2},{8,12},{10,14},{12,8},{14,10},{17,21},{19,... | collective-permute-start | bytes 1179656 | tf_op jit(solution)/shard_map/ppermute | solution.py:32
  444.1 5.5 collective-permute-start.34
  445.9 4.4 collective-permute-start.33
  447.6 14.3 %collective-permute-start.39 = (bf16[384,512]{0,1:T(8,128)(2,1)S(1)}, bf16[384,512]{0,1:T(8,128)(2,1)S(1)}, u32[]{:S(2)}, u32[]{:S(2)}) collective-permute-start(bf16[384,512]{0,1:T(8,128)(2,1)S(1)} %copy-done.18), channel_id=1, source_target_pairs={{0,6},{2,4},{4,2},{6,0},{8,14},{10,12},{12,10},{14,8},{17,23},{19,... | collective-permute-start | bytes 1179656 | tf_op jit(solution)/shard_map/ppermute | solution.py:32
  449.6 5.2 collective-permute-start.38
  450.3 5.2 collective-permute-start.37
  451.0 5.2 collective-permute-start.36
  454.2 7.8 %collective-permute-start.42 = (bf16[384,128]{0,1:T(8,128)(2,1)S(1)}, bf16[384,128]{0,1:T(8,128)(2,1)S(1)}, u32[]{:S(2)}, u32[]{:S(2)}) collective-permute-start(bf16[384,128]{0,1:T(8,128)(2,1)S(1)} %get-tuple-element.60), channel_id=1, source_target_pairs={{1,7},{3,5},{5,3},{7,1},{9,15},{11,13},{13,11},{15,9},{16,22},{18,... | collective-permute-start | bytes 294920 | tf_op jit(solution)/shard_map/ppermute | solution.py:32
  454.9 7.1 %collective-permute-start.41 = (bf16[384,128]{0,1:T(8,128)(2,1)S(1)}, bf16[384,128]{0,1:T(8,128)(2,1)S(1)}, u32[]{:S(2)}, u32[]{:S(2)}) collective-permute-start(bf16[384,128]{0,1:T(8,128)(2,1)S(1)} %get-tuple-element.56), channel_id=1, source_target_pairs={{1,7},{3,5},{5,3},{7,1},{9,15},{11,13},{13,11},{15,9},{16,22},{18,... | collective-permute-start | bytes 294920 | tf_op jit(solution)/shard_map/ppermute | solution.py:32
  455.6 6.4 %collective-permute-start.40 = (bf16[384,256]{0,1:T(8,128)(2,1)S(1)}, bf16[384,256]{0,1:T(8,128)(2,1)S(1)}, u32[]{:S(2)}, u32[]{:S(2)}) collective-permute-start(bf16[384,256]{0,1:T(8,128)(2,1)S(1)} %get-tuple-element.50), channel_id=1, source_target_pairs={{1,7},{3,5},{5,3},{7,1},{9,15},{11,13},{13,11},{15,9},{16,22},{18,... | collective-permute-start | bytes 589832 | tf_op jit(solution)/shard_map/ppermute | solution.py:32
  495.8 33.0 %collective-permute-start.44 = (f32[36,384]{1,0:T(8,128)S(1)}, f32[36,384]{1,0:T(8,128)}, u32[]{:S(2)}, u32[]{:S(2)}) collective-permute-start(f32[36,384]{1,0:T(8,128)S(1)} %concatenate.50), channel_id=1, source_target_pairs={{0,1},{1,0},{2,3},{3,2},{4,5},{5,4},{6,7},{7,6},{8,9},{9,8},{10,11... | collective-permute-start | bytes 165896 | tf_op jit(solution)/shard_map/ppermute | solution.py:32
  542.0 5.6 collective-permute-start.46
  547.6 5.0 collective-permute-start.47
  552.6 7.1 %collective-permute-start.48 = (f32[32,1024]{1,0:T(8,128)S(1)}, f32[32,1024]{1,0:T(8,128)S(1)}, u32[]{:S(2)}, u32[]{:S(2)}) collective-permute-start(f32[32,1024]{1,0:T(8,128)S(1)} %add.197), channel_id=1, source_target_pairs={{0,16},{1,17},{2,18},{3,19},{4,20},{5,21},{6,22},{7,23},{8,24},{9,... | collective-permute-start | bytes 393224 | tf_op jit(solution)/shard_map/ppermute | solution.py:32
  564.1 5.7 collective-permute-start.50
  (29 other events, 605.2 us)
